TPU v7x, 32 devices: a whole 2x2x4 slice. The times are simulated.
32 devices in a mesh: parts: 2 (over x), section: 16 (over z, y, core).
Axes of the slice: x: 2, y: 2, z: 4, core: 2. Of those that a mesh axis runs over, the one named last changes fastest.
Arguments:
- activations: bfloat16 [16, 256, 4, 4096], P('section', 'parts'), parts along dimension 1, may hold values from -6 to 6
- out_grads: bfloat16 [16, 256, 4, 1024], P('section', 'parts'), parts along dimension 1, may hold values from -6 to 6
- in_proj: bfloat16 [16, 16, 4096], P('section'), as said below
- out_proj: bfloat16 [16, 16, 1024], P('section'), as said below
- queries: bfloat16 [16, 256, 256], P('section'), as said below
- assignment: int32 [256], P('parts'), parts along dimension 0, may hold values from 0 to 127, each once
Outputs:
- scores: float32 [256, 256], P(('parts', 'section')), parts along dimension 0
There are 2 independent parts, one for each index of `parts`. A program takes and returns all parts, laid end to end along the dimension named above; an argument that names none is the same for every part. Nothing has to cross between parts.
Inputs may be any that keep to these rules, and one draw needn't show every extreme that they name: `assignment`: a permutation of the 128 examples. `in_proj`: entries at indices that differ by a multiple of 16 are equal. `out_proj`: entries at indices that differ by a multiple of 16 are equal. `queries`: entries at indices that differ by a multiple of 16 are equal.
All inputs are finite; a program needn't handle non-finite values.
Results may differ from a plain program's by a relative error of at most 0.01.
Values may be sent and summed in bfloat16 or wider, within the bound.
A program may use at most 64 MiB of HBM per device.

v0:
```python
import jax
import jax.numpy as jnp
from jax import lax
from jax.sharding import PartitionSpec as P


def shards(activations, out_grads, in_proj, out_proj, queries, assignment):
    act_proj = jnp.einsum(
        "etd,kd->etk", activations[0], in_proj[0], preferred_element_type=jnp.float32
    )
    grad_proj = jnp.einsum(
        "etd,kd->etk", out_grads[0], out_proj[0], preferred_element_type=jnp.float32
    )
    outer_sum = jnp.einsum("eta,etb->eab", grad_proj, act_proj)
    features = outer_sum.reshape(outer_sum.shape[0], -1).astype(jnp.bfloat16)
    ex_group = activations.shape[1]
    example_count = assignment.shape[0]
    groups = example_count // ex_group
    group_id = lax.axis_index("section") // (lax.axis_size("section") // groups)
    local_index = assignment - group_id * ex_group
    inside = (local_index >= 0) & (local_index < ex_group)
    picked = jnp.clip(local_index, 0, ex_group - 1)
    partial_scores = jnp.einsum(
        "ef,qf->eq", features, queries[0], preferred_element_type=jnp.float32
    )
    widened = features.astype(jnp.float32)
    squares = jnp.sum(widened * widened, axis=1)
    score_terms = jnp.where(inside[:, None], jnp.take(partial_scores, picked, axis=0), 0.0)
    square_terms = jnp.where(inside, jnp.take(squares, picked, axis=0), 0.0)
    totals, norm_sq = (
        lax.psum_scatter(score_terms, "section", scatter_dimension=0, tiled=True),
        lax.psum_scatter(square_terms, "section", scatter_dimension=0, tiled=True),
    )
    return totals * lax.rsqrt(norm_sq + 1e-06)[:, None]


def solution(mesh):
    return jax.shard_map(
        shards,
        mesh=mesh,
        in_specs=(
            P("section", "parts", None, None),
            P("section", "parts", None, None),
            P("section", None, None),
            P("section", None, None),
            P("section", None, None),
            P("parts"),
        ),
        out_specs=P(("parts", "section"), None),
        check_vma=False,
    )
```

profile of v0, /device:TPU:0, one launch (start us, length us, event | category | flops | bytes accessed | tf_op | source)
XLA Modules:
  0.0 85.5 jit_solution(2986021400055052223)
XLA Ops:
  6.5 0.0 copy-start
  6.5 0.0 copy-start.1
  6.5 0.0 reduce-scatter.2.cloned.1.call-start
  6.5 1.9 %fusion.2 = bf16[128,4,16]{0,2,1:T(8,128)(2,1)S(1)} fusion(bf16[128,4,1024]{2,1,0:T(4,128)(2,1)} %bitcast.20, bf16[1,16,1024]{2,1,0:T(8,128)(2,1)} %param.9), kind=kOutput, calls=%fused_computation.4 | convolution fusion | flops 16777216 | bytes 1097728 | tf_op jit(solution)/shard_map/etd,kd->etk/dot_general | solution.py:11
  8.5 0.1 copy.15
  8.6 0.0 copy-start.2
  8.6 6.6 %fusion = bf16[128,4,16]{0,2,1:T(8,128)(2,1)S(1)} fusion(bf16[128,4,4096]{2,1,0:T(4,128)(2,1)} %bitcast.19, bf16[1,16,4096]{2,1,0:T(8,128)(2,1)} %param.8), kind=kOutput, calls=%fused_computation.2 | convolution fusion | flops 67108864 | bytes 4341760 | tf_op jit(solution)/shard_map/etd,kd->etk/dot_general | solution.py:8
  15.3 0.1 copy.16
  15.4 0.4 fusion.9
  15.8 0.4 copy.17
  16.3 0.0 copy-done.1
  16.3 0.1 multiply_reduce_fusion
  16.3 0.0 copy-done
  16.3 0.2 fusion.4
  16.5 0.8 gather_fusion
  17.3 1.2 %gather_fusion.1 = f32[128]{0:T(128)S(1)} fusion(f32[128]{0:T(128)S(1)} %multiply_reduce_fusion, s32[1024]{0:T(1024)S(1)} %pad_clamp_fusion), kind=kCustom, calls=%fused_computation.1 | custom fusion | bytes 1536 | tf_op jit(solution)/shard_map/jit(_take)/gather | solution.py:29
  18.6 0.7 select_select_fusion
  19.3 0.0 reduce-scatter.2.cloned.1.call-update
  19.3 0.0 copy-done.2
  19.3 0.6 dynamic-slice
  20.6 35.0 %all-reduce = f32[128]{0:T(128)S(1)} all-reduce(f32[128]{0:T(128)S(1)} %get-tuple-element.5), channel_id=3, replica_groups=mesh['parts'=2,'section'=16] {'section'}, use_global_device_ids=true, to_apply=%region_2.3.clone | all-reduce | flops 128 | bytes 1024
  55.5 0.1 fusion.8
  55.6 21.6 %reduce-scatter.2.cloned.1.call-done = f32[8,256]{1,0:T(8,128)} async-done(((f32[128,256]{1,0:T(8,128)}), f32[8,256]{1,0:T(8,128)}) %reduce-scatter.2.cloned.1.call-update) | async-done | bytes 8208 | tf_op jit(solution)/shard_map/reduce_scatter | solution.py:31
  77.3 1.4 %broadcast_multiply_fusion = f32[8,256]{1,0:T(8,128)} fusion(f32[8,256]{1,0:T(8,128)} %reduce-scatter.2.cloned.1.call-done, f32[8]{0:T(128)S(1)} %fusion.8), kind=kLoop, calls=%fused_computation.13 | loop fusion | flops 2048 | bytes 16416 | tf_op jit(solution)/shard_map/mul | solution.py:34
  (3 shorter events, 0.0 us)
Async XLA Ops:
  6.5 9.8 %copy-start = (bf16[1,256,256]{2,1,0:T(8,128)(2,1)S(1)}, bf16[1,256,256]{2,1,0:T(8,128)(2,1)}, u32[]{:S(2)}) copy-start(bf16[1,256,256]{2,1,0:T(8,128)(2,1)} %param.10) | copy-start | bytes 393220
  6.5 9.7 %copy-start.1 = (s32[128]{0:T(128)S(1)}, s32[128]{0:T(128)}, u32[]{:S(2)}) copy-start(s32[128]{0:T(128)} %param.11) | copy-start | bytes 1540
  6.5 70.7 %reduce-scatter.2.cloned.1.call-start = ((), (), s32[]{:S(2)}) async-start(), calls=%async_computation.1 | async-start | bytes 139264 | tf_op jit(solution)/shard_map/reduce_scatter | solution.py:31
  8.6 10.7 %copy-start.2 = (u32[32]{0:T(128)S(1)}, u32[32]{0:T(128)}, u32[]{:S(2)}) copy-start(u32[32]{0:T(128)} %constant.63) | copy-start | bytes 388
Sparse Core Ops, SparseCore 0:
  19.4 57.7 reduce-scatter.1
where the time goes:
time: 85.7 us; the launch traced here: 85.5 us
  blocking collectives  35 us (41%)
  waiting for transfers between devices  21.7 us (25%)
  between operations  14.1 us (16%)
  matrix products  9.16 us (11%)
  local copies, waits for them, and re-layouts  3.3 us (4%)
  other arithmetic  2.26 us (3%)
    unnamed x1, blocking collectives  35 us
    reduce_scatter x1, waiting for transfers between devices, shards(): lax.psum_scatter(score_terms, 'section', scatter_dimension=0, tiled=True)  21.6 us
    dot_general x1, matrix products, shards(): jnp.einsum('etd,kd->etk', activations[0], in_proj[0], preferred_element_t...  6.65 us
    dot_general x1, matrix products, shards(): jnp.einsum('etd,kd->etk', out_grads[0], out_proj[0], preferred_element_ty...  1.94 us
  transfers between devices with their start and end apart: 1, of which 1 were waited for; matrix products, arithmetic and copies ran while one was open for 1% of the time, Pallas kernels for 0%

commit v1 on v0

v1 whole, which is shorter than its diff:
```python
import functools

import jax
import jax.numpy as jnp
from jax import lax
from jax.experimental import pallas as pl
from jax.experimental.pallas import tpu as pltpu
from jax.sharding import PartitionSpec as P

LANES = 128
SUB = 8
CHUNK = 32
NT = (((1,), (1,)), ((), ()))


def dot_nt(a, b):
    return lax.dot_general(a, b, NT, preferred_element_type=jnp.float32)


def interleaved(weight):
    k, d = weight.shape
    steps = d // (4 * LANES)
    rows = []
    for c in range(4):
        cols = [weight[:, (4 * j + c) * LANES : (4 * j + c + 1) * LANES] for j in range(steps)]
        rows.append(jnp.concatenate(cols, axis=1))
    return jnp.concatenate(rows, axis=0)


def project(ref, start, size, weight):
    steps = ref.shape[1]
    width = weight.shape[0]
    tiles = [ref[pl.ds(start, size), j].reshape(size * 16, LANES) for j in range(steps)]
    acc = dot_nt(jnp.concatenate(tiles, axis=1), weight).reshape(size, 2, SUB, width)
    lane = lax.broadcasted_iota(jnp.int32, (1, SUB, width), 2) // (width // 4)
    sub = lax.broadcasted_iota(jnp.int32, (1, SUB, width), 1) // 4
    both = jnp.where(lane < 2, acc[:, 0], acc[:, 1])
    both = jnp.where(lane % 2 == sub, both, 0.0)
    both = both + pltpu.roll(both, 4, 1)
    both = both.reshape(size // 2, 2, SUB, width)
    pair = jnp.where(sub == 0, both[:, 0], both[:, 1])
    return pair.reshape(size * 4, width).astype(jnp.bfloat16)


def kernel(
    n,
    layers,
    act_hbm,
    grad_hbm,
    in_hbm,
    out_hbm,
    query_hbm,
    assign_hbm,
    scores_ref,
    act,
    grad,
    w_in,
    w_out,
    query,
    assign,
    spread,
    feats,
    send,
    recv,
    sq_send,
    sq_recv,
    act_sem,
    load_sem,
    send_sem,
    recv_sem,
):
    me = lax.axis_index("section")
    part = lax.axis_index("parts")
    ex = act.shape[0]
    rows = assign.shape[1]
    chunks = ex // CHUNK
    k_in = w_in.shape[0]
    k_out = w_out.shape[0]

    loads = []
    for i, (src, dst) in enumerate(
        ((out_hbm, w_out), (grad_hbm, grad), (in_hbm, w_in))
    ):
        loads.append(pltpu.make_async_copy(src, dst, load_sem.at[i]))
    acts = [
        pltpu.make_async_copy(
            act_hbm.at[pl.ds(i * CHUNK, CHUNK)], act.at[pl.ds(i * CHUNK, CHUNK)], act_sem.at[i]
        )
        for i in range(chunks)
    ]
    late = [
        pltpu.make_async_copy(assign_hbm, assign, load_sem.at[3]),
        pltpu.make_async_copy(query_hbm, query, load_sem.at[4]),
    ]
    late[0].start()
    for copy in loads + acts + late[1:]:
        copy.start()

    barrier = pltpu.get_barrier_semaphore()

    @pl.loop(1, n)
    def _(i):
        pl.semaphore_signal(
            barrier, inc=1, device_id=(part, lax.rem(me + i, n)), device_id_type=pl.DeviceIdType.MESH
        )

    late[0].wait()
    first = (me // layers) * ex
    place = lax.broadcasted_iota(jnp.int32, (4 * ex, rows), 0)
    hot = jnp.where(place == (assign[...] - first) * 4, 1.0, 0.0)
    spread[...] = hot.T.astype(jnp.bfloat16)

    def expander(k, other, of_out):
        src = lax.broadcasted_iota(jnp.int32, (4 * k, k_in * k_out), 0) % k
        dst = lax.broadcasted_iota(jnp.int32, (4 * k, k_in * k_out), 1)
        dst = dst // k_in if of_out else dst % k_in
        return jnp.where(src == dst, 1.0, 0.0).astype(jnp.bfloat16)

    over_out = expander(k_out, k_in, True)
    over_in = expander(k_in, k_out, False)

    loads[0].wait()
    loads[1].wait()
    weight_out = interleaved(w_out[...])
    loads[2].wait()
    weight_in = interleaved(w_in[...])
    for i in range(chunks):
        g = jnp.dot(
            project(grad, i * CHUNK, CHUNK, weight_out), over_out, preferred_element_type=jnp.float32
        )
        acts[i].wait()
        a = jnp.dot(
            project(act, i * CHUNK, CHUNK, weight_in), over_in, preferred_element_type=jnp.float32
        )
        y = (g * a).reshape(CHUNK // 2, SUB, k_in * k_out)
        y = y + pltpu.roll(y, 7, 1)
        y = y + pltpu.roll(y, 6, 1)
        feats[pl.ds(4 * i * CHUNK, 4 * CHUNK), :] = y.reshape(4 * CHUNK, k_in * k_out).astype(
            jnp.bfloat16
        )

    picked = jnp.dot(spread[...], feats[...], preferred_element_type=jnp.float32)
    late[1].wait()
    partial = dot_nt(picked.astype(jnp.bfloat16), query[...])
    blocks = partial.reshape(n, rows // n, partial.shape[1])
    half = blocks.shape[2] // 2
    send[...] = jnp.concatenate([blocks[:, :, :half], blocks[:, :, half:]], axis=1).astype(
        jnp.bfloat16
    )
    square = picked * picked
    folded = square[:, :LANES]
    for j in range(1, square.shape[1] // LANES):
        folded = folded + square[:, j * LANES : (j + 1) * LANES]
    sq_send[...] = jnp.sum(folded.T, axis=0, keepdims=True)

    pl.semaphore_wait(barrier, n - 1)

    def copies(i):
        peer = lax.rem(me + i, n)
        target = dict(device_id=(part, peer), device_id_type=pl.DeviceIdType.MESH)
        return (
            pltpu.make_async_remote_copy(
                send.at[peer], recv.at[i], send_sem.at[0], recv_sem.at[0], **target
            ),
            pltpu.make_async_remote_copy(
                sq_send, sq_recv.at[i], send_sem.at[1], recv_sem.at[1], **target
            ),
        )

    @pl.loop(1, n)
    def _(i):
        for copy in copies(i):
            copy.start()

    pltpu.make_async_copy(recv.at[pl.ds(1, n - 1)], recv.at[pl.ds(1, n - 1)], recv_sem.at[0]).wait()
    pltpu.make_async_copy(
        sq_recv.at[pl.ds(1, n - 1)], sq_recv.at[pl.ds(1, n - 1)], recv_sem.at[1]
    ).wait()
    total = jnp.sum(recv[1:].astype(jnp.float32), axis=0) + send[me].astype(jnp.float32)
    norms = jnp.sum(sq_recv[1:], axis=0) + sq_send[...]
    per = rows // n
    column = lax.broadcasted_iota(jnp.int32, (per, rows), 1)
    mine = column == me * per + lax.broadcasted_iota(jnp.int32, (per, rows), 0)
    norm_sq = jnp.sum(jnp.where(mine, norms, 0.0), axis=1, keepdims=True)
    inv_norm = lax.rsqrt(norm_sq + 1e-06)
    scores_ref[:, :half] = total[:per] * inv_norm
    scores_ref[:, half:] = total[per:] * inv_norm
    pltpu.make_async_copy(send.at[pl.ds(1, n - 1)], send.at[pl.ds(1, n - 1)], send_sem.at[0]).wait()
    pltpu.make_async_copy(
        sq_recv.at[pl.ds(1, n - 1)], sq_recv.at[pl.ds(1, n - 1)], send_sem.at[1]
    ).wait()


def by_register(x):
    ex, tok, d = x.shape
    x = x.reshape(ex, tok, d // (4 * LANES), 4, LANES)
    return x.transpose(0, 2, 3, 1, 4).reshape(ex, d // (4 * LANES), 4 * tok, LANES)


def shards(n, activations, out_grads, in_proj, out_proj, queries, assignment):
    act = by_register(activations[0])
    grad = by_register(out_grads[0])
    rows = assignment.shape[0]
    ex = act.shape[0]
    layers = n // (rows // ex)
    k_in = in_proj.shape[1]
    k_out = out_proj.shape[1]
    any_space = pl.BlockSpec(memory_space=pl.ANY)
    bf16 = jnp.bfloat16
    return pl.pallas_call(
        functools.partial(kernel, n, layers),
        out_shape=jax.ShapeDtypeStruct((rows // n, queries.shape[1]), jnp.float32),
        in_specs=[any_space] * 6,
        out_specs=pl.BlockSpec(memory_space=pltpu.VMEM),
        scratch_shapes=[
            pltpu.VMEM(act.shape, bf16),
            pltpu.VMEM(grad.shape, bf16),
            pltpu.VMEM(in_proj.shape[1:], bf16),
            pltpu.VMEM(out_proj.shape[1:], bf16),
            pltpu.VMEM(queries.shape[1:], bf16),
            pltpu.VMEM((1, rows), jnp.int32),
            pltpu.VMEM((rows, 4 * ex), bf16),
            pltpu.VMEM((4 * ex, k_in * k_out), bf16),
            pltpu.VMEM((n, 16, LANES), bf16),
            pltpu.VMEM((n, 16, LANES), bf16),
            pltpu.VMEM((1, rows), jnp.float32),
            pltpu.VMEM((n, 1, rows), jnp.float32),
            pltpu.SemaphoreType.DMA((ex // CHUNK,)),
            pltpu.SemaphoreType.DMA((5,)),
            pltpu.SemaphoreType.DMA((2,)),
            pltpu.SemaphoreType.DMA((2,)),
        ],
        compiler_params=pltpu.CompilerParams(
            collective_id=0, has_side_effects=True, vmem_limit_bytes=56 * 1024 * 1024
        ),
    )(act, grad, in_proj[0], out_proj[0], queries[0], assignment[None, :])


def solution(mesh):
    return jax.shard_map(
        functools.partial(shards, mesh.shape["section"]),
        mesh=mesh,
        in_specs=(
            P("section", "parts", None, None),
            P("section", "parts", None, None),
            P("section", None, None),
            P("section", None, None),
            P("section", None, None),
            P("parts"),
        ),
        out_specs=P(("parts", "section"), None),
        check_vma=False,
    )
```

time: 85.7 us -> 16.5 us (0.19)
  blocking collectives: 35 us -> 0 us
  waiting for transfers between devices: 21.7 us -> 0 us
  Pallas kernels: 0 us -> 15 us
  between operations: 14.1 us -> 0.01 us
  matrix products: 9.16 us -> 0 us
  other arithmetic: 2.26 us -> 0 us
  local copies, waits for them, and re-layouts: 3.3 us -> 1.3 us
    unnamed x1 -> x0, blocking collectives: 35 us -> none
    reduce_scatter x1 -> x0, waiting for transfers between devices: 21.6 us -> none  [shards(): lax.psum_scatter(score_terms, 'section', scatter_dimension=0, tiled=True)]
    pallas_call x0 -> x1, Pallas kernels: none -> 15 us  [shards(): pl.pallas_call(functools.partial(kernel, n, layers), out_shape=jax.ShapeD...]
    dot_general x4 -> x0, matrix products: 9.16 us -> none  [the longest x1 6.65 us: shards(): jnp.einsum('etd,kd->etk', activations[0], in_proj[0], preferred_element_t...]
    gather x2 -> x0, local copies, waits for them, and re-layouts: 1.99 us -> none  [the longest x1 1.23 us: shards(): square_terms = jnp.where(inside, jnp.take(squares, picked, axis=0), 0.0)]
    mul x1 -> x0, other arithmetic: 1.36 us -> none  [shards(): return totals * lax.rsqrt(norm_sq + 1e-06)[:, None]]
  transfers between devices with their start and end apart: 1 -> 0, of which waited for: 1 -> 0; matrix products, arithmetic and copies ran while one was open for 1% -> 0% of each run, Pallas kernels for 0% -> 0%
where the time goes in v1:
time: 16.5 us; the launch traced here: 16.3 us
  Pallas kernels  15 us (91%)
  local copies, waits for them, and re-layouts  1.3 us (8%)
    pallas_call x1, Pallas kernels, shards(): pl.pallas_call(functools.partial(kernel, n, layers), out_shape=jax.ShapeD...  15 us
    unnamed x1, local copies, waits for them, and re-layouts  1.3 us

profile of v1, /device:TPU:0, one launch (start us, length us, event | category | flops | bytes accessed | tf_op | source)
XLA Modules:
  0.0 16.3 jit_solution(9947274255722869286)
XLA Ops:
  0.0 15.0 %shard_map.64 = f32[8,256]{1,0:T(8,128)} custom-call(bf16[128,8,16,128]{3,2,1,0:T(8,128)(2,1)} %bitcast.14, bf16[128,2,16,128]{3,2,1,0:T(8,128)(2,1)} %bitcast.15, bf16[16,4096]{1,0:T(8,128)(2,1)} %bitcast.16, bf16[16,1024]{1,0:T(8,128)(2,1)} %bitcast.18, bf16[256,256]{1,0:T(8,128)(2,1)} %bitcast.17, s32[1,128]{1,0:T(1,128)} %bitcast.19), custom_call_target="tpu_custom_call" | custom-call | tf_op jit(solution)/shard_map/pallas_call | solution.py:210
  15.0 1.3 %copy.10 = f32[8,256]{1,0:T(8,128)} copy(f32[8,256]{1,0:T(8,128)} %shard_map.64) | data formatting | bytes 16384

commit v2 on v1

--- a/solution.py
+++ b/solution.py
@@ -9,7 +9,7 @@
 
 LANES = 128
 SUB = 8
-CHUNK = 32
+SHARES = (8,)
 NT = (((1,), (1,)), ((), ()))
 
 
@@ -59,11 +59,10 @@
     query,
     assign,
     spread,
-    feats,
+    wide,
+    proj,
     send,
     recv,
-    sq_send,
-    sq_recv,
     act_sem,
     load_sem,
     send_sem,
@@ -73,7 +72,9 @@
     part = lax.axis_index("parts")
     ex = act.shape[0]
     rows = assign.shape[1]
-    chunks = ex // CHUNK
+    per = rows // n
+    sizes = [ex * share // 8 for share in SHARES]
+    starts = [sum(sizes[:i]) for i in range(len(sizes))]
     k_in = w_in.shape[0]
     k_out = w_out.shape[0]
 
@@ -84,9 +85,9 @@
         loads.append(pltpu.make_async_copy(src, dst, load_sem.at[i]))
     acts = [
         pltpu.make_async_copy(
-            act_hbm.at[pl.ds(i * CHUNK, CHUNK)], act.at[pl.ds(i * CHUNK, CHUNK)], act_sem.at[i]
+            act_hbm.at[pl.ds(at, size)], act.at[pl.ds(at, size)], act_sem.at[i]
         )
-        for i in range(chunks)
+        for i, (at, size) in enumerate(zip(starts, sizes))
     ]
     late = [
         pltpu.make_async_copy(assign_hbm, assign, load_sem.at[3]),
@@ -120,75 +121,55 @@
     over_in = expander(k_in, k_out, False)
 
     loads[0].wait()
-    loads[1].wait()
-    weight_out = interleaved(w_out[...])
     loads[2].wait()
     weight_in = interleaved(w_in[...])
-    for i in range(chunks):
-        g = jnp.dot(
-            project(grad, i * CHUNK, CHUNK, weight_out), over_out, preferred_element_type=jnp.float32
-        )
+    weight_out = interleaved(w_out[...])
+    loads[1].wait()
+    wide[...] = jnp.dot(
+        project(grad, 0, ex, weight_out), over_out, preferred_element_type=jnp.float32
+    )
+    for i, (at, size) in enumerate(zip(starts, sizes)):
         acts[i].wait()
-        a = jnp.dot(
-            project(act, i * CHUNK, CHUNK, weight_in), over_in, preferred_element_type=jnp.float32
-        )
-        y = (g * a).reshape(CHUNK // 2, SUB, k_in * k_out)
-        y = y + pltpu.roll(y, 7, 1)
-        y = y + pltpu.roll(y, 6, 1)
-        feats[pl.ds(4 * i * CHUNK, 4 * CHUNK), :] = y.reshape(4 * CHUNK, k_in * k_out).astype(
-            jnp.bfloat16
-        )
-
-    picked = jnp.dot(spread[...], feats[...], preferred_element_type=jnp.float32)
+        proj[pl.ds(4 * at, 4 * size), :] = project(act, at, size, weight_in)
     late[1].wait()
+    y = wide[...] * jnp.dot(proj[...], over_in, preferred_element_type=jnp.float32)
+    y = y.reshape(ex // 2, SUB, k_in * k_out)
+    y = y + pltpu.roll(y, 7, 1)
+    y = y + pltpu.roll(y, 6, 1)
+    features = y.reshape(4 * ex, k_in * k_out).astype(jnp.bfloat16)
+
+    picked = jnp.dot(spread[...], features, preferred_element_type=jnp.float32)
     partial = dot_nt(picked.astype(jnp.bfloat16), query[...])
-    blocks = partial.reshape(n, rows // n, partial.shape[1])
+    blocks = partial.reshape(n, per, partial.shape[1])
     half = blocks.shape[2] // 2
-    send[...] = jnp.concatenate([blocks[:, :, :half], blocks[:, :, half:]], axis=1).astype(
-        jnp.bfloat16
-    )
-    square = picked * picked
-    folded = square[:, :LANES]
-    for j in range(1, square.shape[1] // LANES):
-        folded = folded + square[:, j * LANES : (j + 1) * LANES]
-    sq_send[...] = jnp.sum(folded.T, axis=0, keepdims=True)
+    square = jnp.sum(picked * picked, axis=1, keepdims=True)
+    square = jnp.broadcast_to(square, (rows, LANES)).reshape(n, per, LANES)
+    high = square.astype(jnp.bfloat16).astype(jnp.float32)
+    send[...] = jnp.concatenate(
+        [blocks[:, :, :half], blocks[:, :, half:], high, square - high], axis=1
+    ).astype(jnp.bfloat16)
 
     pl.semaphore_wait(barrier, n - 1)
-
-    def copies(i):
-        peer = lax.rem(me + i, n)
-        target = dict(device_id=(part, peer), device_id_type=pl.DeviceIdType.MESH)
-        return (
-            pltpu.make_async_remote_copy(
-                send.at[peer], recv.at[i], send_sem.at[0], recv_sem.at[0], **target
-            ),
-            pltpu.make_async_remote_copy(
-                sq_send, sq_recv.at[i], send_sem.at[1], recv_sem.at[1], **target
-            ),
-        )
 
     @pl.loop(1, n)
     def _(i):
-        for copy in copies(i):
-            copy.start()
-
-    pltpu.make_async_copy(recv.at[pl.ds(1, n - 1)], recv.at[pl.ds(1, n - 1)], recv_sem.at[0]).wait()
-    pltpu.make_async_copy(
-        sq_recv.at[pl.ds(1, n - 1)], sq_recv.at[pl.ds(1, n - 1)], recv_sem.at[1]
-    ).wait()
+        peer = lax.rem(me + i, n)
+        pltpu.make_async_remote_copy(
+            send.at[peer],
+            recv.at[i],
+            send_sem,
+            recv_sem,
+            device_id=(part, peer),
+            device_id_type=pl.DeviceIdType.MESH,
+        ).start()
+
+    others = pl.ds(1, n - 1)
+    pltpu.make_async_copy(recv.at[others], recv.at[others], recv_sem).wait()
     total = jnp.sum(recv[1:].astype(jnp.float32), axis=0) + send[me].astype(jnp.float32)
-    norms = jnp.sum(sq_recv[1:], axis=0) + sq_send[...]
-    per = rows // n
-    column = lax.broadcasted_iota(jnp.int32, (per, rows), 1)
-    mine = column == me * per + lax.broadcasted_iota(jnp.int32, (per, rows), 0)
-    norm_sq = jnp.sum(jnp.where(mine, norms, 0.0), axis=1, keepdims=True)
-    inv_norm = lax.rsqrt(norm_sq + 1e-06)
+    inv_norm = lax.rsqrt(total[2 * per : 3 * per] + total[3 * per :] + 1e-06)
     scores_ref[:, :half] = total[:per] * inv_norm
-    scores_ref[:, half:] = total[per:] * inv_norm
-    pltpu.make_async_copy(send.at[pl.ds(1, n - 1)], send.at[pl.ds(1, n - 1)], send_sem.at[0]).wait()
-    pltpu.make_async_copy(
-        sq_recv.at[pl.ds(1, n - 1)], sq_recv.at[pl.ds(1, n - 1)], send_sem.at[1]
-    ).wait()
+    scores_ref[:, half:] = total[per : 2 * per] * inv_norm
+    pltpu.make_async_copy(send.at[others], send.at[others], send_sem).wait()
 
 
 def by_register(x):
@@ -209,7 +190,7 @@
     bf16 = jnp.bfloat16
     return pl.pallas_call(
         functools.partial(kernel, n, layers),
-        out_shape=jax.ShapeDtypeStruct((rows // n, queries.shape[1]), jnp.float32),
+        out_shape=pltpu.VMEM((rows // n, queries.shape[1]), jnp.float32),
         in_specs=[any_space] * 6,
         out_specs=pl.BlockSpec(memory_space=pltpu.VMEM),
         scratch_shapes=[
@@ -220,15 +201,14 @@
             pltpu.VMEM(queries.shape[1:], bf16),
             pltpu.VMEM((1, rows), jnp.int32),
             pltpu.VMEM((rows, 4 * ex), bf16),
-            pltpu.VMEM((4 * ex, k_in * k_out), bf16),
-            pltpu.VMEM((n, 16, LANES), bf16),
-            pltpu.VMEM((n, 16, LANES), bf16),
-            pltpu.VMEM((1, rows), jnp.float32),
-            pltpu.VMEM((n, 1, rows), jnp.float32),
-            pltpu.SemaphoreType.DMA((ex // CHUNK,)),
+            pltpu.VMEM((4 * ex, k_in * k_out), jnp.float32),
+            pltpu.VMEM((4 * ex, 4 * k_in), bf16),
+            pltpu.VMEM((n, 4 * (rows // n), LANES), bf16),
+            pltpu.VMEM((n, 4 * (rows // n), LANES), bf16),
+            pltpu.SemaphoreType.DMA((len(SHARES),)),
             pltpu.SemaphoreType.DMA((5,)),
-            pltpu.SemaphoreType.DMA((2,)),
-            pltpu.SemaphoreType.DMA((2,)),
+            pltpu.SemaphoreType.DMA,
+            pltpu.SemaphoreType.DMA,
         ],
         compiler_params=pltpu.CompilerParams(
             collective_id=0, has_side_effects=True, vmem_limit_bytes=56 * 1024 * 1024

time: 16.5 us -> 13.3 us (0.81)
  Pallas kernels: 15 us -> 12.5 us
  local copies, waits for them, and re-layouts: 1.3 us -> 0.6 us
    pallas_call x1, Pallas kernels: 15 us -> 12.5 us  [shards(): pl.pallas_call(functools.partial(kernel, n, layers), out_shape=pltpu.VMEM...]
    unnamed x1, local copies, waits for them, and re-layouts: 1.3 us -> 0.6 us
where the time goes in v2:
time: 13.3 us; the launch traced here: 13.1 us
  Pallas kernels  12.5 us (94%)
  local copies, waits for them, and re-layouts  0.6 us (5%)
    pallas_call x1, Pallas kernels, shards(): pl.pallas_call(functools.partial(kernel, n, layers), out_shape=pltpu.VMEM...  12.5 us
    unnamed x1, local copies, waits for them, and re-layouts  0.6 us

profile of v2, /device:TPU:0, one launch (start us, length us, event | category | flops | bytes accessed | tf_op | source)
XLA Modules:
  0.0 13.1 jit_solution(5161031675520899324)
XLA Ops:
  0.0 12.5 %shard_map.64 = f32[8,256]{1,0:T(8,128)S(1)} custom-call(bf16[128,8,16,128]{3,2,1,0:T(8,128)(2,1)} %bitcast.14, bf16[128,2,16,128]{3,2,1,0:T(8,128)(2,1)} %bitcast.15, bf16[16,4096]{1,0:T(8,128)(2,1)} %bitcast.16, bf16[16,1024]{1,0:T(8,128)(2,1)} %bitcast.18, bf16[256,256]{1,0:T(8,128)(2,1)} %bitcast.17, s32[1,128]{1,0:T(1,128)} %bitcast.19), custom_call_target="tpu_custom_call" | custom-call | tf_op jit(solution)/shard_map/pallas_call | solution.py:191
  12.5 0.6 %copy.10 = f32[8,256]{1,0:T(8,128)} copy(f32[8,256]{1,0:T(8,128)S(1)} %shard_map.64) | data formatting | bytes 16384

commit v3 on v2

--- a/solution.py
+++ b/solution.py
@@ -9,7 +9,8 @@
 
 LANES = 128
 SUB = 8
-SHARES = (8,)
+ACT_STEP = 64
+GRAD_STEP = 32
 NT = (((1,), (1,)), ((), ()))
 
 
@@ -63,7 +64,6 @@
     proj,
     send,
     recv,
-    act_sem,
     load_sem,
     send_sem,
     recv_sem,
@@ -73,28 +73,20 @@
     ex = act.shape[0]
     rows = assign.shape[1]
     per = rows // n
-    sizes = [ex * share // 8 for share in SHARES]
-    starts = [sum(sizes[:i]) for i in range(len(sizes))]
     k_in = w_in.shape[0]
     k_out = w_out.shape[0]
 
     loads = []
     for i, (src, dst) in enumerate(
-        ((out_hbm, w_out), (grad_hbm, grad), (in_hbm, w_in))
+        ((out_hbm, w_out), (grad_hbm, grad), (in_hbm, w_in), (act_hbm, act))
     ):
         loads.append(pltpu.make_async_copy(src, dst, load_sem.at[i]))
-    acts = [
-        pltpu.make_async_copy(
-            act_hbm.at[pl.ds(at, size)], act.at[pl.ds(at, size)], act_sem.at[i]
-        )
-        for i, (at, size) in enumerate(zip(starts, sizes))
-    ]
     late = [
-        pltpu.make_async_copy(assign_hbm, assign, load_sem.at[3]),
-        pltpu.make_async_copy(query_hbm, query, load_sem.at[4]),
+        pltpu.make_async_copy(assign_hbm, assign, load_sem.at[4]),
+        pltpu.make_async_copy(query_hbm, query, load_sem.at[5]),
     ]
     late[0].start()
-    for copy in loads + acts + late[1:]:
+    for copy in loads + late[1:]:
         copy.start()
 
     barrier = pltpu.get_barrier_semaphore()
@@ -125,12 +117,13 @@
     weight_in = interleaved(w_in[...])
     weight_out = interleaved(w_out[...])
     loads[1].wait()
-    wide[...] = jnp.dot(
-        project(grad, 0, ex, weight_out), over_out, preferred_element_type=jnp.float32
-    )
-    for i, (at, size) in enumerate(zip(starts, sizes)):
-        acts[i].wait()
-        proj[pl.ds(4 * at, 4 * size), :] = project(act, at, size, weight_in)
+    for at in range(0, ex, GRAD_STEP):
+        wide[pl.ds(4 * at, 4 * GRAD_STEP), :] = jnp.dot(
+            project(grad, at, GRAD_STEP, weight_out), over_out, preferred_element_type=jnp.float32
+        )
+    loads[3].wait()
+    for at in range(0, ex, ACT_STEP):
+        proj[pl.ds(4 * at, 4 * ACT_STEP), :] = project(act, at, ACT_STEP, weight_in)
     late[1].wait()
     y = wide[...] * jnp.dot(proj[...], over_in, preferred_element_type=jnp.float32)
     y = y.reshape(ex // 2, SUB, k_in * k_out)
@@ -205,8 +198,7 @@
             pltpu.VMEM((4 * ex, 4 * k_in), bf16),
             pltpu.VMEM((n, 4 * (rows // n), LANES), bf16),
             pltpu.VMEM((n, 4 * (rows // n), LANES), bf16),
-            pltpu.SemaphoreType.DMA((len(SHARES),)),
-            pltpu.SemaphoreType.DMA((5,)),
+            pltpu.SemaphoreType.DMA((6,)),
             pltpu.SemaphoreType.DMA,
             pltpu.SemaphoreType.DMA,
         ],

time: 13.3 us -> 12.9 us (0.970)
  Pallas kernels: 12.5 us -> 12.2 us
    pallas_call x1, Pallas kernels: 12.5 us -> 12.2 us  [shards(): pl.pallas_call(functools.partial(kernel, n, layers), out_shape=pltpu.VMEM...]
where the time goes in v3:
time: 12.9 us; the launch traced here: 12.8 us
  Pallas kernels  12.2 us (95%)
  local copies, waits for them, and re-layouts  0.6 us (5%)
    pallas_call x1, Pallas kernels, shards(): pl.pallas_call(functools.partial(kernel, n, layers), out_shape=pltpu.VMEM...  12.2 us
    unnamed x1, local copies, waits for them, and re-layouts  0.6 us

profile of v3, /device:TPU:0, one launch (start us, length us, event | category | flops | bytes accessed | tf_op | source)
XLA Modules:
  0.0 12.8 jit_solution(13751165662463595478)
XLA Ops:
  0.0 12.2 %shard_map.64 = f32[8,256]{1,0:T(8,128)S(1)} custom-call(bf16[128,8,16,128]{3,2,1,0:T(8,128)(2,1)} %bitcast.14, bf16[128,2,16,128]{3,2,1,0:T(8,128)(2,1)} %bitcast.15, bf16[16,4096]{1,0:T(8,128)(2,1)} %bitcast.16, bf16[16,1024]{1,0:T(8,128)(2,1)} %bitcast.18, bf16[256,256]{1,0:T(8,128)(2,1)} %bitcast.17, s32[1,128]{1,0:T(1,128)} %bitcast.19), custom_call_target="tpu_custom_call" | custom-call | tf_op jit(solution)/shard_map/pallas_call | solution.py:184
  12.2 0.6 %copy.10 = f32[8,256]{1,0:T(8,128)} copy(f32[8,256]{1,0:T(8,128)S(1)} %shard_map.64) | data formatting | bytes 16384

commit v4 on v3

--- a/solution.py
+++ b/solution.py
@@ -113,14 +113,14 @@
     over_in = expander(k_in, k_out, False)
 
     loads[0].wait()
-    loads[2].wait()
-    weight_in = interleaved(w_in[...])
     weight_out = interleaved(w_out[...])
     loads[1].wait()
     for at in range(0, ex, GRAD_STEP):
         wide[pl.ds(4 * at, 4 * GRAD_STEP), :] = jnp.dot(
             project(grad, at, GRAD_STEP, weight_out), over_out, preferred_element_type=jnp.float32
         )
+    loads[2].wait()
+    weight_in = interleaved(w_in[...])
     loads[3].wait()
     for at in range(0, ex, ACT_STEP):
         proj[pl.ds(4 * at, 4 * ACT_STEP), :] = project(act, at, ACT_STEP, weight_in)

time: 12.9 us -> 12.9 us (level)
  no operation moved by 1% of the time
where the time goes in v4:
time: 12.9 us; the launch traced here: 12.8 us
  Pallas kernels  12.2 us (95%)
  local copies, waits for them, and re-layouts  0.6 us (5%)
    pallas_call x1, Pallas kernels, shards(): pl.pallas_call(functools.partial(kernel, n, layers), out_shape=pltpu.VMEM...  12.2 us
    unnamed x1, local copies, waits for them, and re-layouts  0.6 us

profile of v4, /device:TPU:0, one launch (start us, length us, event | category | flops | bytes accessed | tf_op | source)
XLA Modules:
  0.0 12.8 jit_solution(2558634959873004109)
XLA Ops:
  0.0 12.2 %shard_map.64 = f32[8,256]{1,0:T(8,128)S(1)} custom-call(bf16[128,8,16,128]{3,2,1,0:T(8,128)(2,1)} %bitcast.14, bf16[128,2,16,128]{3,2,1,0:T(8,128)(2,1)} %bitcast.15, bf16[16,4096]{1,0:T(8,128)(2,1)} %bitcast.16, bf16[16,1024]{1,0:T(8,128)(2,1)} %bitcast.18, bf16[256,256]{1,0:T(8,128)(2,1)} %bitcast.17, s32[1,128]{1,0:T(1,128)} %bitcast.19), custom_call_target="tpu_custom_call" | custom-call | tf_op jit(solution)/shard_map/pallas_call | solution.py:184
  12.2 0.6 %copy.10 = f32[8,256]{1,0:T(8,128)} copy(f32[8,256]{1,0:T(8,128)S(1)} %shard_map.64) | data formatting | bytes 16384
